TPU v7x, 128 devices: a whole 4x4x4 slice. The times are simulated.
128 devices in a mesh: rep: 2 (over core), dp: 8 (over y_hi, x), tensor: 8 (over z, y_lo).
Axes of the slice: x: 4, y: 4 (y_hi: 2, y_lo: 2; y = y_hi * 2 + y_lo), z: 4, core: 2. Of those that a mesh axis runs over, the one named last changes fastest.
Arguments:
- frames: bfloat16 [64, 384, 8, 128], P(('rep', 'dp'), 'tensor'), may hold values from -6 to 6
- weight: bfloat16 [384, 3, 3, 3, 384], P('tensor'), may hold values from -0.0625 to 0.0625
- cotangent: bfloat16 [64, 384, 8, 128], P(('rep', 'dp'), 'tensor'), may hold values from -6 to 6
- prev_owner: int32 [16], replicated, may hold values from -1 to 15, as said below
- lengths: int32 [16], replicated, may hold values from 1 to 4, as said below
Outputs:
- output: bfloat16 [64, 384, 8, 128], P(('rep', 'dp'), 'tensor')
- input_grad: float32 [64, 384, 8, 128], P(('rep', 'dp'), 'tensor')
- weight_grad: float32 [384, 3, 3, 3, 384], P('tensor')
Inputs may be any that keep to these rules, and one draw needn't show every extreme that they name: `prev_owner`: each segment index appears at most once; segment 0 of every clip has -1; clips form chains without loops. A segment named in prev_owner has lengths 4; only a clip's last segment may be shorter.
All inputs are finite; a program needn't handle non-finite values.
Results may differ from a plain program's by a relative error of at most 0.0034.
Values may be sent and summed in bfloat16 or wider, within the bound.
No kernel may reach another device: no remote copies, remote signals or barrier semaphores. Data moves between devices by JAX's collectives and lax.ppermute only.
A program may use at most 128 MiB of HBM per device.

v0:
```python
import math

import jax
import jax.numpy as jnp
from jax import lax
from jax.experimental import pallas as pl
from jax.experimental.pallas import tpu as pltpu
from jax.sharding import PartitionSpec as P

BF16 = jnp.bfloat16
F32 = jnp.float32
VMEM_LIMIT = 56 * 1024 * 1024
ANY = pl.BlockSpec(memory_space=pl.ANY)
VMEM = pl.BlockSpec(memory_space=pltpu.VMEM)
SMEM = pl.BlockSpec(memory_space=pltpu.SMEM)

PLACES = ((0, 0), (0, 1), (1, 0), (3, 0), (1, 1), (3, 1), (2, 0), (2, 1))


def tensor_index(ring, pair):
    return ring * 2 + pair


class Group:
    def __init__(self, name, index_of, coords):
        self.name = name
        self.index_of = index_of
        me = lax.axis_index(name)
        self.ring, self.pair = coords(me)
        cells = [(r, p) for r in range(4) for p in range(2)]
        self.perm_up = [(index_of(r, p), index_of((r + 1) % 4, p)) for r, p in cells]
        self.perm_down = [(index_of(r, p), index_of((r + 3) % 4, p)) for r, p in cells]
        self.perm_swap = [(index_of(r, p), index_of(r, 1 - p)) for r, p in cells]

    def up(self, x):
        return lax.ppermute(x, self.name, self.perm_up)

    def down(self, x):
        return lax.ppermute(x, self.name, self.perm_down)

    def swap(self, x):
        return lax.ppermute(x, self.name, self.perm_swap)

    def absolute(self):
        return [self.index_of((self.ring + dr) % 4, self.pair ^ dp) for dr, dp in PLACES]

    def gather(self, x):
        half = x.shape[0] // 2
        following, prev, pair = lax.optimization_barrier((self.down(x), self.up(x), self.swap(x)))
        pair_next = self.swap(following)
        pair_prev = self.up(pair)
        second = self.down(following)
        far_a = self.down(pair_next[:half])
        far_b = self.up(pair_prev[half:])
        return [x, pair, following, prev, pair_next, pair_prev, second, far_a, far_b]

    def scatter_sum(self, parts):
        own, pair, following, prev, pair_next, pair_prev, second, far_a, far_b = parts
        from_prev = self.down(prev)
        in_a = self.up(far_a)
        in_b = self.down(far_b)
        pair_next = added(pair_next, jnp.concatenate([in_a, jnp.zeros_like(in_a)], 0))
        pair_prev = added(pair_prev, jnp.concatenate([jnp.zeros_like(in_b), in_b], 0))
        got_up = self.up(second)
        got_swap = self.swap(pair_next)
        got_down = self.down(pair_prev)
        last_up = self.up(added(following, got_swap, got_up))
        last_swap = self.swap(added(pair, got_down))
        return sum(x.astype(F32) for x in (own, from_prev, last_up, last_swap))


def added(*terms):
    return sum(x.astype(F32) for x in terms).astype(BF16)


def shifted(x, by):
    lanes = x.shape[-1]
    column = lax.broadcasted_iota(jnp.int32, x.shape, x.ndim - 1) % 128
    rolled = pltpu.roll(x, by % lanes, x.ndim - 1)
    edge = 0 if by == 1 else 127
    return jnp.where(column == edge, 0.0, rolled)


def fill_taps(live_ref, m_ref, head_ref, taps):
    rows, width, lanes = m_ref.shape
    frames = taps.shape[2] // 128
    taps[0] = jnp.zeros(taps.shape[1:], BF16)
    taps[rows + 1] = jnp.zeros(taps.shape[1:], BF16)
    for h in range(rows):
        whole = jnp.concatenate([m_ref[h], head_ref[h]], 1).astype(F32)
        wide = jnp.concatenate(
            [
                jnp.where(live_ref[f] > 0, whole[:, f * 128 : f * 128 + 128], 0.0)
                for f in range(frames)
            ],
            1,
        )
        taps[h + 1, 0:width] = shifted(wide, -1).astype(BF16)
        taps[h + 1, width : 2 * width] = wide.astype(BF16)
        taps[h + 1, 2 * width : 3 * width] = shifted(wide, 1).astype(BF16)


def input_grad_kernel(place_ref, live_ref, m_ref, head_ref, w_ref, *rest):
    outs, (taps, wt, parts, sems) = rest[:9], rest[9:]
    rows, width, lanes = m_ref.shape
    half = rows // 2
    fill_taps(live_ref, m_ref, head_ref, taps)
    depth = 3 * 3 * width
    for a in range(3):
        block = jnp.concatenate([w_ref[a * 3 + b] for b in range(3)], 0)
        wt[:, a * depth : (a + 1) * depth] = block.T

    copies = []
    for h in range(rows):
        stack = jnp.reshape(taps[h : h + 3], (depth, taps.shape[2]))
        for start in range(0, lanes, 256):
            rhs = jnp.concatenate(
                [stack[:, (2 - a) * 128 + start : (2 - a) * 128 + start + 256] for a in range(3)], 0
            )
            total = jnp.dot(wt[...], rhs, preferred_element_type=F32).astype(BF16)
            for t in range(8):
                parts[t, h, :, start : start + 256] = total[t * width : (t + 1) * width]
        if h % half == half - 1:
            part, first = h // half, h + 1 - half
            for r in range(8):
                source = parts.at[place_ref[r], first : first + half]
                target = outs[r].at[first : first + half] if r < 7 else outs[7 + part]
                copies.append(pltpu.make_async_copy(source, target, sems.at[part, r]))
                copies[-1].start()
    for copy in copies:
        copy.wait()


def pick_kernel(row_ref, from_ref, own_ref, other_ref, out_ref):
    for d in range(out_ref.shape[0]):
        own, other = own_ref[row_ref[d]], other_ref[row_ref[d]]
        chosen = jnp.where(from_ref[d] == 1, own, other)
        out_ref[d] = jnp.where(from_ref[d] == 0, jnp.zeros_like(chosen), chosen)


CHUNK = 2


def start_loads(place_ref, blocks, x, sems):
    rows, width = blocks[0].shape[0], blocks[0].shape[1]
    half = rows // 2
    x[0] = jnp.zeros(x.shape[1:], BF16)
    x[rows + 1] = jnp.zeros(x.shape[1:], BF16)
    lists = []
    for part in range(rows // CHUNK):
        first = part * CHUNK
        copies = []
        for r in range(8):
            channel = pl.ds(pl.multiple_of(place_ref[r] * width, 16), width)
            block, skip = (blocks[r], 0) if r < 7 else (blocks[7 + first // half], first // half * half)
            copies.append(
                pltpu.make_async_copy(
                    block.at[first - skip : first - skip + CHUNK],
                    x.at[first + 1 : first + 1 + CHUNK, channel],
                    sems.at[part, r],
                )
            )
            copies[-1].start()
        lists.append(copies)
    return lists


def wait_for(copies):
    for copy in copies:
        copy.wait()


def forward_kernel(place_ref, after_ref, *rest):
    del after_ref
    blocks, (w_ref, out_ref, carry_ref, x, sems) = rest[:9], rest[9:]
    rows, width, lanes = out_ref.shape
    loads = start_loads(place_ref, blocks, x, sems)
    lhs = jnp.concatenate(
        [jnp.concatenate([w_ref[a * 3 + 2 - b] for a in range(3)], 0) for b in range(3)], 1
    )
    wait_for(loads[0])
    for h in range(rows):
        if (h + 1) % CHUNK == 0 and h + 1 < rows:
            wait_for(loads[(h + 1) // CHUNK])
        stack = jnp.reshape(x[h : h + 3], (3 * x.shape[1], lanes))
        y = jnp.dot(lhs, stack, preferred_element_type=F32)
        sums = []
        for e in range(3):
            frames = []
            for g in range(lanes // 128 + 2):
                terms = []
                for a in range(3):
                    f = g + a - 2
                    if 0 <= f < lanes // 128:
                        row = (a * 3 + e) * width
                        terms.append(y[row : row + width, f * 128 : f * 128 + 128])
                total = terms[0]
                for term in terms[1:]:
                    total = total + term
                frames.append(total)
            sums.append(jnp.concatenate(frames, 1))
        result = sums[1] + shifted(sums[0], 1) + shifted(sums[2], -1)
        out_ref[h] = result[:, :lanes]
        carry_ref[h, :width] = result[:, lanes : lanes + 128].astype(BF16)
        carry_ref[h, width:] = result[:, lanes + 128 :].astype(BF16)


def kernel_grad_kernel(place_ref, live_ref, rep_ref, after_ref, *rest):
    del after_ref
    blocks, (m_ref, head_ref, mine_ref, theirs_ref, x, taps, total, result, sems, out_sems) = rest[:9], rest[9:]
    rows, width, lanes = m_ref.shape
    loads = start_loads(place_ref, blocks, x, sems)
    fill_taps(live_ref, m_ref, head_ref, taps)
    depth = 9 * width
    result[9 * depth :, :] = jnp.zeros((result.shape[0] - 9 * depth, 128), F32)
    for h in range(rows):
        if h % CHUNK == 0:
            wait_for(loads[h // CHUNK])
        stack = jnp.reshape(taps[h : h + 3], (depth, taps.shape[2]))
        right = x[h + 1]
        for a in range(3):
            left = stack[:, (2 - a) * 128 : (2 - a) * 128 + lanes]
            product = lax.dot_general(
                left, right, (((1,), (1,)), ((), ())), preferred_element_type=F32
            )
            if h == 0:
                total[a] = product
            elif h < rows - 1:
                total[a] += product
            else:
                product = total[a] + product
                for block in range(3):
                    row = (a * 3 + block) * depth
                    result[row : row + depth, :] = product[:, block * 128 : block * 128 + 128]
    half = result.shape[0] // 2
    copies = []
    for slot, (target, rep) in enumerate(((theirs_ref, 1 - rep_ref[0]), (mine_ref, rep_ref[0]))):
        source = result.at[pl.ds(pl.multiple_of(rep * half, 16), half)]
        copies.append(pltpu.make_async_copy(source, target, out_sems.at[slot]))
        copies[-1].start()
    wait_for(copies)


def params():
    return pltpu.CompilerParams(vmem_limit_bytes=VMEM_LIMIT)


def cost(flops, size):
    return pl.CostEstimate(flops=flops, bytes_accessed=size, transcendentals=0)


FLOPS = 2 * 27 * 48 * 384 * 4096


def input_partials(place, live, m, head, weight):
    rows, width, lanes = m.shape
    channels = weight.shape[2]
    whole = jax.ShapeDtypeStruct((rows, width, lanes), BF16)
    half = jax.ShapeDtypeStruct((rows // 2, width, lanes), BF16)
    return pl.pallas_call(
        input_grad_kernel,
        out_shape=[whole] * 7 + [half] * 2,
        in_specs=[SMEM, SMEM, VMEM, VMEM, VMEM],
        out_specs=[ANY] * 9,
        scratch_shapes=[
            pltpu.VMEM((rows + 2, 3 * width, lanes + 256), BF16),
            pltpu.VMEM((channels, 27 * width), BF16),
            pltpu.VMEM((8, rows, width, lanes), BF16),
            pltpu.SemaphoreType.DMA((2, 8)),
        ],
        compiler_params=params(),
        cost_estimate=cost(FLOPS, 5_000_000),
        name="input_partials",
    )(place, live, m, head, weight)


def pick(row, origin, own, other):
    return pl.pallas_call(
        pick_kernel,
        out_shape=jax.ShapeDtypeStruct(own.shape, own.dtype),
        in_specs=[SMEM, SMEM, VMEM, VMEM],
        out_specs=VMEM,
        compiler_params=params(),
        name="pick",
    )(row, origin, own, other)


def forward(place, after, blocks, weight):
    rows, width, lanes = blocks[0].shape
    channels = weight.shape[2]
    return pl.pallas_call(
        forward_kernel,
        out_shape=[
            jax.ShapeDtypeStruct((rows, width, lanes), F32),
            jax.ShapeDtypeStruct((rows, 2 * width, 128), BF16),
        ],
        in_specs=[SMEM] + [ANY] * 10 + [VMEM],
        out_specs=[VMEM, VMEM],
        scratch_shapes=[
            pltpu.VMEM((rows + 2, channels, lanes), BF16),
            pltpu.SemaphoreType.DMA((rows // CHUNK, 8)),
        ],
        compiler_params=params(),
        cost_estimate=cost(FLOPS, 5_000_000),
        name="forward",
    )(place, after, *blocks, weight)


def kernel_grad(place, live, rep, after, blocks, m, head):
    rows, width, lanes = m.shape
    channels = 8 * width
    return pl.pallas_call(
        kernel_grad_kernel,
        out_shape=[jax.ShapeDtypeStruct((2048, 128), F32)] * 2,
        in_specs=[SMEM] * 3 + [ANY] * 10 + [VMEM, VMEM],
        out_specs=[ANY, ANY],
        scratch_shapes=[
            pltpu.VMEM((rows + 2, channels, lanes), BF16),
            pltpu.VMEM((rows + 2, 3 * width, lanes + 256), BF16),
            pltpu.VMEM((3, 9 * width, channels), F32),
            pltpu.VMEM((4096, 128), F32),
            pltpu.SemaphoreType.DMA((rows // CHUNK, 8)),
            pltpu.SemaphoreType.DMA((2,)),
        ],
        compiler_params=params(),
        cost_estimate=cost(FLOPS, 6_000_000),
        name="kernel_grad",
    )(place, live, rep, after, *blocks, m, head)


def to_rows(x):
    f, c, h, w = x.shape
    return x.transpose(2, 1, 0, 3).reshape(h, c, f * w)


def from_rows(x):
    h, c, lanes = x.shape
    return x.reshape(h, c, lanes // 128, 128).transpose(2, 1, 0, 3)


def core_swap(x):
    return lax.ppermute(x, "rep", [(0, 1), (1, 0)])


def exchange(x):
    return lax.all_to_all(x, "dp", 0, 0, tiled=True)


def handed_on(own, source):
    rep = lax.axis_index("rep")
    wanted = lax.dynamic_slice_in_dim(source, rep * 8, 8, 0)
    row = jnp.maximum(wanted, 0) % 8
    origin = jnp.where(wanted < 0, 0, jnp.where(wanted // 8 == rep, 1, 2)).astype(jnp.int32)
    return pick(row, origin, own, core_swap(own))


def first_exchange(mine, theirs, payload):
    pair = (mine + core_swap(theirs)).astype(BF16).reshape(8, 256, 128)
    return jnp.concatenate([pair, payload], 1)


def second_exchange(spread, scale, source):
    rep = lax.axis_index("rep")
    handed = handed_on(spread[:, 256:], source)
    share = (jnp.sum(spread[:, :256].astype(F32), 0) * scale).astype(BF16)
    share = jnp.broadcast_to(share[None], (8, 256, 128))
    spread = exchange(jnp.concatenate([share, handed], 1))
    half = spread[:, :256].reshape(2048, 128)
    there = core_swap(half)
    low = jnp.where(rep == 0, half, there)
    high = jnp.where(rep == 0, there, half)
    return jnp.concatenate([low, high], 0), spread[:, 256:]


def per_device(frames, weight, cotangent, prev_owner, lengths):
    seg_len, width, height, columns = frames.shape
    channels = weight.shape[4]
    rep, me = lax.axis_index("rep"), lax.axis_index("dp")
    member = rep * 8 + me
    tensor = Group("tensor", tensor_index, lambda i: (i // 2, i % 2))
    place = jnp.stack(tensor.absolute()).astype(jnp.int32)
    segments = jnp.arange(prev_owner.shape[0], dtype=jnp.int32)
    follows = prev_owner[None, :] == segments[:, None]
    follower = jnp.max(jnp.where(follows, segments[None, :], -1), 1)

    x = to_rows(frames)
    m = to_rows(cotangent)
    rows = weight.transpose(1, 2, 3, 0, 4)[:, ::-1].reshape(9, 3 * width, channels)

    payload, x = lax.optimization_barrier((m[:, :, :256], x))
    payload = exchange(payload)
    blocks = tensor.gather(x)
    head = exchange(handed_on(payload, follower))
    keep = jnp.arange(seg_len) < lengths[member]
    keep_head = jnp.arange(2) < lengths[jnp.maximum(follower[member], 0)]
    live = jnp.concatenate([keep, keep_head]).astype(jnp.int32)

    partials = input_partials(place, live, m, head, rows)
    partials, blocks = lax.optimization_barrier((partials, blocks))
    mine, theirs = kernel_grad(place, live, rep.astype(jnp.int32)[None], partials[0], blocks, m, head)
    conv, carry = forward(place, theirs, blocks, rows)
    spread = first_exchange(mine, theirs, carry)
    input_grad = from_rows(tensor.scatter_sum(partials))

    cells = prev_owner.shape[0] * seg_len * height * columns
    conv = conv.reshape(height, width, seg_len, columns).transpose(2, 1, 0, 3)
    spread, conv = lax.optimization_barrier((exchange(spread), conv))
    total, received = second_exchange(spread, 1.0 / math.sqrt(cells), prev_owner)
    total = total[: 81 * width].reshape(3, 3, 3, 3, width, 128)
    weight_grad = total[:, :, ::-1].transpose(4, 0, 2, 3, 1, 5).reshape(weight.shape).astype(F32)

    received = received.reshape(height, 2, width, columns).transpose(1, 2, 0, 3).astype(F32)
    conv = conv + jnp.concatenate([received, jnp.zeros_like(received)], 0)
    output = jnp.where(keep[:, None, None, None], conv, 0.0).astype(BF16)
    return (output, input_grad, weight_grad)


def solution(mesh):
    split = P(("rep", "dp"), "tensor", None, None)
    kernel = P("tensor", None, None, None, None)
    return jax.shard_map(
        per_device,
        mesh=mesh,
        in_specs=(split, kernel, split, P(), P()),
        out_specs=(split, split, kernel),
        check_vma=False,
    )
```

profile of v0, /device:TPU:1, one launch (start us, length us, event | category | flops | bytes accessed | tf_op | source)
XLA Modules:
  0.0 132.0 jit_solution(11219004343090281917)
XLA Ops:
  0.7 1.3 copy.20
  2.1 1.5 %copy.19 = bf16[8,48,4,128]{3,2,1,0:T(4,128)(2,1)S(1)} copy(bf16[8,48,4,128]{3,0,1,2:T(8,128)(2,1)} %bitcast.47) | data formatting | bytes 786432 | tf_op jit(solution)/shard_map/transpose | solution.py:333
  4.6 2.1 %collective-permute-start.3 = (bf16[8,48,512]{2,1,0:T(8,128)(2,1)S(1)}, bf16[8,48,512]{2,1,0:T(8,128)(2,1)}, u32[]{:S(2)}, u32[]{:S(2)}) collective-permute-start(bf16[8,48,512]{2,1,0:T(8,128)(2,1)S(1)} %reshape.48.rest_0_), channel_id=1, source_target_pairs={{0,1},{1,0},{2,3},{3,2},{4,5},{5,4},{6,7},{7,6},{8,9},{9,8},{10,11... | collective-permute-start | bytes 1179656 | tf_op jit(solution)/shard_map/ppermute | solution.py:42
  6.7 1.6 %collective-permute-start.2 = (bf16[8,48,512]{2,1,0:T(8,128)(2,1)S(1)}, bf16[8,48,512]{2,1,0:T(8,128)(2,1)S(1)}, u32[]{:S(2)}, u32[]{:S(2)}) collective-permute-start(bf16[8,48,512]{2,1,0:T(8,128)(2,1)S(1)} %reshape.48.rest_0_), channel_id=1, source_target_pairs={{0,2},{1,3},{2,4},{3,5},{4,6},{5,7},{6,0},{7,1},{8,10},{9,11},{10,... | collective-permute-start | bytes 1179656 | tf_op jit(solution)/shard_map/ppermute | solution.py:36
  8.4 2.1 %collective-permute-start.1 = (bf16[8,48,512]{2,1,0:T(8,128)(2,1)S(1)}, bf16[8,48,512]{2,1,0:T(8,128)(2,1)}, u32[]{:S(2)}, u32[]{:S(2)}) collective-permute-start(bf16[8,48,512]{2,1,0:T(8,128)(2,1)S(1)} %reshape.48.rest_0_), channel_id=1, source_target_pairs={{0,6},{1,7},{2,0},{3,1},{4,2},{5,3},{6,4},{7,5},{8,14},{9,15},{10,... | collective-permute-start | bytes 1179656 | tf_op jit(solution)/shard_map/ppermute | solution.py:39
  10.5 6.4 %all-to-all-start = ((bf16[8,48,256]{2,1,0:T(8,128)(2,1)}), bf16[8,48,256]{2,1,0:T(8,128)(2,1)S(1)}, u32[]{:S(2)}, u32[]{:S(2)}) async-start(bf16[8,48,256]{2,1,0:T(8,128)(2,1)} %slice.32), calls=%async_computation | async-start | bytes 393216 | tf_op jit(solution)/shard_map/all_to_all | solution.py:346
  18.9 5.3 %all-to-all-done.own_ref = bf16[8,48,256]{2,1,0:T(8,128)(2,1)S(1)} async-done(((bf16[8,48,256]{2,1,0:T(8,128)(2,1)}), bf16[8,48,256]{2,1,0:T(8,128)(2,1)S(1)}, u32[]{:S(2)}, u32[]{:S(2)}) %all-to-all-start) | async-done | bytes 196640 | tf_op jit(solution)/shard_map/all_to_all | solution.py:346
  24.2 2.6 %collective-permute-start = (bf16[8,48,256]{2,1,0:T(8,128)(2,1)S(1)}, bf16[8,48,256]{2,1,0:T(8,128)(2,1)S(1)}, u32[]{:S(2)}, u32[]{:S(2)}) collective-permute-start(bf16[8,48,256]{2,1,0:T(8,128)(2,1)S(1)} %all-to-all-done.own_ref), channel_id=1, source_target_pairs={{0,64},{64,0},{1,65},{65,1},{2,66},{66,2},{3,67},{67,3},{4,68},{68... | collective-permute-start | bytes 589832 | tf_op jit(solution)/shard_map/ppermute | solution.py:342
  29.6 1.7 %pick.2 = bf16[8,48,256]{2,1,0:T(8,128)(2,1)} custom-call(s32[8]{0:T(128)} %get-tuple-element.84.row_ref, s32[8]{0:T(128)} %get-tuple-element.83.from_ref, bf16[8,48,256]{2,1,0:T(8,128)(2,1)} %copy-done.4, bf16[8,48,256]{2,1,0:T(8,128)(2,1)} %copy-done.13), custom_call_target="tpu_custom_call" | custom-call | tf_op jit(solution)/shard_map/pick/pallas_call | solution.py:278
  31.3 3.4 %all-to-all-start.1 = ((bf16[8,48,256]{2,1,0:T(8,128)(2,1)}), bf16[8,48,256]{2,1,0:T(8,128)(2,1)S(1)}, u32[]{:S(2)}, u32[]{:S(2)}) async-start(bf16[8,48,256]{2,1,0:T(8,128)(2,1)} %pick.2), calls=%async_computation.1 | async-start | bytes 393216 | tf_op jit(solution)/shard_map/all_to_all | solution.py:346
  35.4 2.7 %collective-permute-start.6 = (bf16[8,48,512]{2,1,0:T(8,128)(2,1)}, bf16[8,48,512]{2,1,0:T(8,128)(2,1)}, u32[]{:S(2)}, u32[]{:S(2)}) collective-permute-start(bf16[8,48,512]{2,1,0:T(8,128)(2,1)} %collective-permute-done.1.rest_2_), channel_id=1, source_target_pairs={{0,6},{1,7},{2,0},{3,1},{4,2},{5,3},{6,4},{7,5},{8,14},{9,15},{10,... | collective-permute-start | bytes 1179656 | tf_op jit(solution)/shard_map/ppermute | solution.py:39
  40.6 2.9 %collective-permute-start.7 = (bf16[4,48,512]{2,1,0:T(8,128)(2,1)S(1)}, bf16[4,48,512]{2,1,0:T(8,128)(2,1)S(1)}, u32[]{:S(2)}, u32[]{:S(2)}) collective-permute-start(bf16[4,48,512]{2,1,0:T(8,128)(2,1)S(1)} %slice.33), channel_id=1, source_target_pairs={{0,6},{1,7},{2,0},{3,1},{4,2},{5,3},{6,4},{7,5},{8,14},{9,15},{10,... | collective-permute-start | bytes 589832 | tf_op jit(solution)/shard_map/ppermute | solution.py:39
  44.2 8.1 %input_partials.1 = (bf16[8,48,512]{2,1,0:T(8,128)(2,1)}, bf16[8,48,512]{2,1,0:T(8,128)(2,1)}, bf16[8,48,512]{2,1,0:T(8,128)(2,1)}, bf16[8,48,512]{2,1,0:T(8,128...) custom-call(s32[8]{0:T(128)} %stack.35.place_ref, ...), custom_call_target="tpu_custom_call" | custom-call | flops 4076863488 | bytes 5000000 | tf_op jit(solution)/shard_map/input_partials/pallas_call | solution.py:260
  53.1 10.5 %kernel_grad.1 = (f32[2048,128]{1,0:T(8,128)}, f32[2048,128]{1,0:T(8,128)}) custom-call(s32[8]{0:T(128)} %stack.35.place_ref, s32[6]{0:T(128)} %add_convert_fusion.5.live_ref, s32[1]{0:T(128)} %bitcast.11.rep_ref, bf16[8,48,512]{2,1,0:T(8,128)(2,1)} %get-tuple-element.55.after_ref, bf16[8,48,512]{2,1,0:T(8,128)(2,1)} %copy-done.7, ...), custom_call_target="tpu_custom_call" | custom-call | flops 4076863488 | bytes 6000000 | tf_op jit(solution)/shard_map/kernel_grad/pallas_call | solution.py:312
  63.6 1.4 %collective-permute-start.9 = (f32[2048,128]{1,0:T(8,128)}, f32[2048,128]{1,0:T(8,128)S(1)}, u32[]{:S(2)}, u32[]{:S(2)}) collective-permute-start(f32[2048,128]{1,0:T(8,128)} %get-tuple-element.66.after_ref), channel_id=1, source_target_pairs={{0,64},{64,0},{1,65},{65,1},{2,66},{66,2},{3,67},{67,3},{4,68},{68... | collective-permute-start | bytes 3145736 | tf_op jit(solution)/shard_map/ppermute | solution.py:342
  65.2 2.5 %collective-permute-start.16 = (bf16[4,48,512]{2,1,0:T(8,128)(2,1)S(1)}, bf16[4,48,512]{2,1,0:T(8,128)(2,1)S(1)}, u32[]{:S(2)}, u32[]{:S(2)}) collective-permute-start(bf16[4,48,512]{2,1,0:T(8,128)(2,1)S(1)} %copy-done.23), channel_id=1, source_target_pairs={{0,6},{1,7},{2,0},{3,1},{4,2},{5,3},{6,4},{7,5},{8,14},{9,15},{10,... | collective-permute-start | bytes 589832 | tf_op jit(solution)/shard_map/ppermute | solution.py:39
  67.7 9.3 %forward.1 = (f32[8,48,512]{2,1,0:T(8,128)}, bf16[8,96,128]{2,1,0:T(8,128)(2,1)}) custom-call(s32[8]{0:T(128)} %stack.35.place_ref, f32[2048,128]{1,0:T(8,128)} %get-tuple-element.66.after_ref, bf16[8,48,512]{2,1,0:T(8,128)(2,1)} %copy-done.7, bf16[8,48,512]{2,1,0:T(8,128)(2,1)} %collective-permute-done.3.rest_1_, ...), custom_call_target="tpu_custom_call" | custom-call | flops 4076863488 | bytes 5000000 | tf_op jit(solution)/shard_map/forward/pallas_call | solution.py:291
  79.3 6.6 %all-to-all-start.2 = ((bf16[8,352,128]{2,1,0:T(8,128)(2,1)}), bf16[8,352,128]{2,1,0:T(8,128)(2,1)S(1)}, u32[]{:S(2)}, u32[]{:S(2)}) async-start(bf16[8,352,128]{2,1,0:T(8,128)(2,1)} %pad_maximum_fusion.1), calls=%async_computation.2 | async-start | bytes 1441792 | tf_op jit(solution)/shard_map/all_to_all | solution.py:346
  86.6 1.5 %collective-permute-start.14 = (bf16[8,48,512]{2,1,0:T(8,128)(2,1)}, bf16[8,48,512]{2,1,0:T(8,128)(2,1)}, u32[]{:S(2)}, u32[]{:S(2)}) collective-permute-start(bf16[8,48,512]{2,1,0:T(8,128)(2,1)} %get-tuple-element.75), channel_id=1, source_target_pairs={{0,2},{1,3},{2,4},{3,5},{4,6},{5,7},{6,0},{7,1},{8,10},{9,11},{10,... | collective-permute-start | bytes 1179656 | tf_op jit(solution)/shard_map/ppermute | solution.py:36
  88.8 1.7 %add_convert_fusion.4 = bf16[8,48,512]{2,1,0:T(8,128)(2,1)} fusion(bf16[8,48,512]{2,1,0:T(8,128)(2,1)S(1)} %copy-done.10, bf16[4,48,512]{2,1,0:T(8,128)(2,1)} %collective-permute-done.12), kind=kLoop, calls=%fused_computation.11 | loop fusion | flops 786432 | bytes 983040 | tf_op jit(solution)/shard_map/convert_element_type | solution.py:73
  90.6 1.6 %collective-permute-start.13 = (bf16[8,48,512]{2,1,0:T(8,128)(2,1)}, bf16[8,48,512]{2,1,0:T(8,128)(2,1)}, u32[]{:S(2)}, u32[]{:S(2)}) collective-permute-start(bf16[8,48,512]{2,1,0:T(8,128)(2,1)} %add_convert_fusion.4), channel_id=1, source_target_pairs={{0,1},{1,0},{2,3},{3,2},{4,5},{5,4},{6,7},{7,6},{8,9},{9,8},{10,11... | collective-permute-start | bytes 1179656 | tf_op jit(solution)/shard_map/ppermute | solution.py:42
  92.1 1.8 %add_convert_fusion.1 = bf16[8,48,512]{2,1,0:T(8,128)(2,1)} fusion(bf16[8,48,512]{2,1,0:T(8,128)(2,1)} %collective-permute-done.17, bf16[8,48,512]{2,1,0:T(8,128)(2,1)S(1)} %copy-done.9), kind=kLoop, calls=%fused_computation.8 | loop fusion | flops 786432 | bytes 1179648 | tf_op jit(solution)/shard_map/convert_element_type | solution.py:73
  94.0 5.7 %all-to-all-done.2 = bf16[8,352,128]{2,1,0:T(8,128)(2,1)S(1)} async-done(((bf16[8,352,128]{2,1,0:T(8,128)(2,1)}), bf16[8,352,128]{2,1,0:T(8,128)(2,1)S(1)}, u32[]{:S(2)}, u32[]{:S(2)}) %all-to-all-start.2) | async-done | bytes 720928 | tf_op jit(solution)/shard_map/all_to_all | solution.py:346
  102.5 1.8 %pick.3 = bf16[8,96,128]{2,1,0:T(8,128)(2,1)} custom-call(s32[8]{0:T(128)} %get-tuple-element.82.row_ref, s32[8]{0:T(128)} %get-tuple-element.81.from_ref, bf16[8,96,128]{2,1,0:T(8,128)(2,1)} %copy-done.5, bf16[8,96,128]{2,1,0:T(8,128)(2,1)} %copy-done.14), custom_call_target="tpu_custom_call" | custom-call | tf_op jit(solution)/shard_map/pick/pallas_call | solution.py:278
  104.5 1.8 %pad_maximum_fusion.2 = bf16[8,352,128]{2,1,0:T(8,128)(2,1)} fusion(bf16[8,96,128]{2,1,0:T(8,128)(2,1)} %pick.3, bf16[8,256,128]{2,1,0:T(8,128)(2,1)S(1)} %broadcast_in_dim.54), kind=kLoop, calls=%fused_computation.14 | loop fusion | flops 1441792 | bytes 1441792 | tf_op jit(solution)/shard_map/concatenate | solution.py:367
  106.3 3.7 %all-to-all-start.3 = ((bf16[8,352,128]{2,1,0:T(8,128)(2,1)}), bf16[8,352,128]{2,1,0:T(8,128)(2,1)S(1)}, u32[]{:S(2)}, u32[]{:S(2)}) async-start(bf16[8,352,128]{2,1,0:T(8,128)(2,1)} %pad_maximum_fusion.2), calls=%async_computation.3 | async-start | bytes 1441792 | tf_op jit(solution)/shard_map/all_to_all | solution.py:346
  110.0 1.3 add_convert_fusion.3
  111.3 1.5 %collective-permute-start.15 = (bf16[8,48,512]{2,1,0:T(8,128)(2,1)S(1)}, bf16[8,48,512]{2,1,0:T(8,128)(2,1)}, u32[]{:S(2)}, u32[]{:S(2)}) collective-permute-start(bf16[8,48,512]{2,1,0:T(8,128)(2,1)S(1)} %add_convert_fusion.3), channel_id=1, source_target_pairs={{0,2},{1,3},{2,4},{3,5},{4,6},{5,7},{6,0},{7,1},{8,10},{9,11},{10,... | collective-permute-start | bytes 1179656 | tf_op jit(solution)/shard_map/ppermute | solution.py:36
  112.8 11.0 %all-to-all-done.3 = bf16[8,352,128]{2,1,0:T(8,128)(2,1)S(1)} async-done(((bf16[8,352,128]{2,1,0:T(8,128)(2,1)}), bf16[8,352,128]{2,1,0:T(8,128)(2,1)S(1)}, u32[]{:S(2)}, u32[]{:S(2)}) %all-to-all-start.3) | async-done | bytes 720928 | tf_op jit(solution)/shard_map/all_to_all | solution.py:346
  126.9 1.3 %copy.30 = f32[8,48,4,128]{3,0,1,2:T(8,128)} copy(f32[8,48,4,128]{3,2,1,0:T(4,128)S(1)} %reshape.52) | data formatting | bytes 1572864 | tf_op jit(solution)/shard_map/reshape | solution.py:338
  129.3 1.3 broadcast_select_fusion.1
  130.6 1.4 %copy_bitcast_fusion = f32[48,3,3,3,384]{4,0,3,2,1:T(8,128)} fusion(bf16[3,3,3,3,48,128]{5,4,3,2,1,0:T(8,128)(2,1)S(1)} %bitcast.37), kind=kLoop, calls=%fused_computation | loop fusion | flops 497664 | bytes 2985984 | tf_op jit(solution)/shard_map/convert_element_type | solution.py:410
  (109 shorter events, 20.7 us)
Async XLA Ops:
  0.6 16.2 %copy-start.19 = (s32[16]{0:T(128)S(1)}, s32[16]{0:T(128)}, u32[]{:S(2)}) copy-start(s32[16]{0:T(128)} %param.8) | copy-start | bytes 196
  0.6 17.6 %copy-start.18 = (s32[16]{0:T(128)S(1)}, s32[16]{0:T(128)}, u32[]{:S(2)}) copy-start(s32[16]{0:T(128)} %param.9) | copy-start | bytes 196
  2.0 36.7 %copy-start.1 = (bf16[48,3,3,3,384]{4,0,3,2,1:T(8,128)(2,1)S(1)}, bf16[48,3,3,3,384]{4,0,3,2,1:T(8,128)(2,1)}, u32[]{:S(2)}) copy-start(bf16[48,3,3,3,384]{4,0,3,2,1:T(8,128)(2,1)} %param.6) | copy-start | bytes 2985988
  2.1 37.6 %copy-start.7 = (bf16[8,48,512]{2,1,0:T(8,128)(2,1)}, bf16[8,48,512]{2,1,0:T(8,128)(2,1)S(1)}, u32[]{:S(2)}) copy-start(bf16[8,48,512]{2,1,0:T(8,128)(2,1)S(1)} %reshape.48.rest_0_) | copy-start | bytes 1179652
  3.8 35.9 %copy-start.2 = (bf16[8,48,512]{2,1,0:T(8,128)(2,1)}, bf16[8,48,512]{2,1,0:T(8,128)(2,1)S(1)}, u32[]{:S(2)}) copy-start(bf16[8,48,512]{2,1,0:T(8,128)(2,1)S(1)} %reshape.47.m_ref.rest_9_) | copy-start | bytes 1179652
  4.6 22.2 %collective-permute-start.3 = (bf16[8,48,512]{2,1,0:T(8,128)(2,1)S(1)}, bf16[8,48,512]{2,1,0:T(8,128)(2,1)}, u32[]{:S(2)}, u32[]{:S(2)}) collective-permute-start(bf16[8,48,512]{2,1,0:T(8,128)(2,1)S(1)} %reshape.48.rest_0_), channel_id=1, source_target_pairs={{0,1},{1,0},{2,3},{3,2},{4,5},{5,4},{6,7},{7,6},{8,9},{9,8},{10,11... | collective-permute-start | bytes 1179656 | tf_op jit(solution)/shard_map/ppermute | solution.py:42
  6.7 20.1 %collective-permute-start.2 = (bf16[8,48,512]{2,1,0:T(8,128)(2,1)S(1)}, bf16[8,48,512]{2,1,0:T(8,128)(2,1)S(1)}, u32[]{:S(2)}, u32[]{:S(2)}) collective-permute-start(bf16[8,48,512]{2,1,0:T(8,128)(2,1)S(1)} %reshape.48.rest_0_), channel_id=1, source_target_pairs={{0,2},{1,3},{2,4},{3,5},{4,6},{5,7},{6,0},{7,1},{8,10},{9,11},{10,... | collective-permute-start | bytes 1179656 | tf_op jit(solution)/shard_map/ppermute | solution.py:36
  8.4 19.2 %collective-permute-start.1 = (bf16[8,48,512]{2,1,0:T(8,128)(2,1)S(1)}, bf16[8,48,512]{2,1,0:T(8,128)(2,1)}, u32[]{:S(2)}, u32[]{:S(2)}) collective-permute-start(bf16[8,48,512]{2,1,0:T(8,128)(2,1)S(1)} %reshape.48.rest_0_), channel_id=1, source_target_pairs={{0,6},{1,7},{2,0},{3,1},{4,2},{5,3},{6,4},{7,5},{8,14},{9,15},{10,... | collective-permute-start | bytes 1179656 | tf_op jit(solution)/shard_map/ppermute | solution.py:39
  10.5 13.7 %all-to-all-start = ((bf16[8,48,256]{2,1,0:T(8,128)(2,1)}), bf16[8,48,256]{2,1,0:T(8,128)(2,1)S(1)}, u32[]{:S(2)}, u32[]{:S(2)}) async-start(bf16[8,48,256]{2,1,0:T(8,128)(2,1)} %slice.32), calls=%async_computation | async-start | bytes 393216 | tf_op jit(solution)/shard_map/all_to_all | solution.py:346
  24.2 4.8 %collective-permute-start = (bf16[8,48,256]{2,1,0:T(8,128)(2,1)S(1)}, bf16[8,48,256]{2,1,0:T(8,128)(2,1)S(1)}, u32[]{:S(2)}, u32[]{:S(2)}) collective-permute-start(bf16[8,48,256]{2,1,0:T(8,128)(2,1)S(1)} %all-to-all-done.own_ref), channel_id=1, source_target_pairs={{0,64},{64,0},{1,65},{65,1},{2,66},{66,2},{3,67},{67,3},{4,68},{68... | collective-permute-start | bytes 589832 | tf_op jit(solution)/shard_map/ppermute | solution.py:342
  27.6 12.8 %collective-permute-start.5 = (bf16[8,48,512]{2,1,0:T(8,128)(2,1)}, bf16[8,48,512]{2,1,0:T(8,128)(2,1)S(1)}, u32[]{:S(2)}, u32[]{:S(2)}) collective-permute-start(bf16[8,48,512]{2,1,0:T(8,128)(2,1)} %collective-permute-done.3.rest_1_), channel_id=1, source_target_pairs={{0,2},{1,3},{2,4},{3,5},{4,6},{5,7},{6,0},{7,1},{8,10},{9,11},{10,... | collective-permute-start | bytes 1179656 | tf_op jit(solution)/shard_map/ppermute | solution.py:36
  27.6 12.9 %collective-permute-start.4 = (bf16[8,48,512]{2,1,0:T(8,128)(2,1)}, bf16[8,48,512]{2,1,0:T(8,128)(2,1)S(1)}, u32[]{:S(2)}, u32[]{:S(2)}) collective-permute-start(bf16[8,48,512]{2,1,0:T(8,128)(2,1)} %collective-permute-done.1.rest_2_), channel_id=1, source_target_pairs={{0,1},{1,0},{2,3},{3,2},{4,5},{5,4},{6,7},{7,6},{8,9},{9,8},{10,11... | collective-permute-start | bytes 1179656 | tf_op jit(solution)/shard_map/ppermute | solution.py:42
  31.3 12.1 %all-to-all-start.1 = ((bf16[8,48,256]{2,1,0:T(8,128)(2,1)}), bf16[8,48,256]{2,1,0:T(8,128)(2,1)S(1)}, u32[]{:S(2)}, u32[]{:S(2)}) async-start(bf16[8,48,256]{2,1,0:T(8,128)(2,1)} %pick.2), calls=%async_computation.1 | async-start | bytes 393216 | tf_op jit(solution)/shard_map/all_to_all | solution.py:346
  35.4 16.9 %collective-permute-start.6 = (bf16[8,48,512]{2,1,0:T(8,128)(2,1)}, bf16[8,48,512]{2,1,0:T(8,128)(2,1)}, u32[]{:S(2)}, u32[]{:S(2)}) collective-permute-start(bf16[8,48,512]{2,1,0:T(8,128)(2,1)} %collective-permute-done.1.rest_2_), channel_id=1, source_target_pairs={{0,6},{1,7},{2,0},{3,1},{4,2},{5,3},{6,4},{7,5},{8,14},{9,15},{10,... | collective-permute-start | bytes 1179656 | tf_op jit(solution)/shard_map/ppermute | solution.py:39
  40.5 11.9 %collective-permute-start.8 = (bf16[4,48,512]{2,1,0:T(8,128)(2,1)S(1)}, bf16[4,48,512]{2,1,0:T(8,128)(2,1)S(1)}, u32[]{:S(2)}, u32[]{:S(2)}) collective-permute-start(bf16[4,48,512]{2,1,0:T(8,128)(2,1)S(1)} %slice.34), channel_id=1, source_target_pairs={{0,2},{1,3},{2,4},{3,5},{4,6},{5,7},{6,0},{7,1},{8,10},{9,11},{10,... | collective-permute-start | bytes 589832 | tf_op jit(solution)/shard_map/ppermute | solution.py:36
  40.6 11.8 %collective-permute-start.7 = (bf16[4,48,512]{2,1,0:T(8,128)(2,1)S(1)}, bf16[4,48,512]{2,1,0:T(8,128)(2,1)S(1)}, u32[]{:S(2)}, u32[]{:S(2)}) collective-permute-start(bf16[4,48,512]{2,1,0:T(8,128)(2,1)S(1)} %slice.33), channel_id=1, source_target_pairs={{0,6},{1,7},{2,0},{3,1},{4,2},{5,3},{6,4},{7,5},{8,14},{9,15},{10,... | collective-permute-start | bytes 589832 | tf_op jit(solution)/shard_map/ppermute | solution.py:39
  63.6 13.4 %copy-start.11 = (bf16[8,48,512]{2,1,0:T(8,128)(2,1)S(1)}, bf16[8,48,512]{2,1,0:T(8,128)(2,1)}, u32[]{:S(2)}) copy-start(bf16[8,48,512]{2,1,0:T(8,128)(2,1)} %get-tuple-element.77) | copy-start | bytes 1179652
  63.6 14.6 %copy-start = (f32[2048,128]{1,0:T(8,128)S(1)}, f32[2048,128]{1,0:T(8,128)}, u32[]{:S(2)}) copy-start(f32[2048,128]{1,0:T(8,128)} %get-tuple-element.65) | copy-start | bytes 3145732
  63.6 14.6 %collective-permute-start.9 = (f32[2048,128]{1,0:T(8,128)}, f32[2048,128]{1,0:T(8,128)S(1)}, u32[]{:S(2)}, u32[]{:S(2)}) collective-permute-start(f32[2048,128]{1,0:T(8,128)} %get-tuple-element.66.after_ref), channel_id=1, source_target_pairs={{0,64},{64,0},{1,65},{65,1},{2,66},{66,2},{3,67},{67,3},{4,68},{68... | collective-permute-start | bytes 3145736 | tf_op jit(solution)/shard_map/ppermute | solution.py:342
  65.0 23.8 %collective-permute-start.12 = (bf16[4,48,512]{2,1,0:T(8,128)(2,1)}, bf16[4,48,512]{2,1,0:T(8,128)(2,1)}, u32[]{:S(2)}, u32[]{:S(2)}) collective-permute-start(bf16[4,48,512]{2,1,0:T(8,128)(2,1)} %get-tuple-element.74), channel_id=1, source_target_pairs={{0,2},{1,3},{2,4},{3,5},{4,6},{5,7},{6,0},{7,1},{8,10},{9,11},{10,... | collective-permute-start | bytes 589832 | tf_op jit(solution)/shard_map/ppermute | solution.py:36
  65.2 11.8 %collective-permute-start.16 = (bf16[4,48,512]{2,1,0:T(8,128)(2,1)S(1)}, bf16[4,48,512]{2,1,0:T(8,128)(2,1)S(1)}, u32[]{:S(2)}, u32[]{:S(2)}) collective-permute-start(bf16[4,48,512]{2,1,0:T(8,128)(2,1)S(1)} %copy-done.23), channel_id=1, source_target_pairs={{0,6},{1,7},{2,0},{3,1},{4,2},{5,3},{6,4},{7,5},{8,14},{9,15},{10,... | collective-permute-start | bytes 589832 | tf_op jit(solution)/shard_map/ppermute | solution.py:39
  77.8 14.3 %collective-permute-start.17 = (bf16[8,48,512]{2,1,0:T(8,128)(2,1)}, bf16[8,48,512]{2,1,0:T(8,128)(2,1)}, u32[]{:S(2)}, u32[]{:S(2)}) collective-permute-start(bf16[8,48,512]{2,1,0:T(8,128)(2,1)} %add_convert_fusion.2), channel_id=1, source_target_pairs={{0,6},{1,7},{2,0},{3,1},{4,2},{5,3},{6,4},{7,5},{8,14},{9,15},{10,... | collective-permute-start | bytes 1179656 | tf_op jit(solution)/shard_map/ppermute | solution.py:39
  79.3 20.4 %all-to-all-start.2 = ((bf16[8,352,128]{2,1,0:T(8,128)(2,1)}), bf16[8,352,128]{2,1,0:T(8,128)(2,1)S(1)}, u32[]{:S(2)}, u32[]{:S(2)}) async-start(bf16[8,352,128]{2,1,0:T(8,128)(2,1)} %pad_maximum_fusion.1), calls=%async_computation.2 | async-start | bytes 1441792 | tf_op jit(solution)/shard_map/all_to_all | solution.py:346
  86.6 38.9 %collective-permute-start.11 = (bf16[8,48,512]{2,1,0:T(8,128)(2,1)}, bf16[8,48,512]{2,1,0:T(8,128)(2,1)S(1)}, u32[]{:S(2)}, u32[]{:S(2)}) collective-permute-start(bf16[8,48,512]{2,1,0:T(8,128)(2,1)} %get-tuple-element.71), channel_id=1, source_target_pairs={{0,6},{1,7},{2,0},{3,1},{4,2},{5,3},{6,4},{7,5},{8,14},{9,15},{10,... | collective-permute-start | bytes 1179656 | tf_op jit(solution)/shard_map/ppermute | solution.py:39
  86.6 23.4 %collective-permute-start.14 = (bf16[8,48,512]{2,1,0:T(8,128)(2,1)}, bf16[8,48,512]{2,1,0:T(8,128)(2,1)}, u32[]{:S(2)}, u32[]{:S(2)}) collective-permute-start(bf16[8,48,512]{2,1,0:T(8,128)(2,1)} %get-tuple-element.75), channel_id=1, source_target_pairs={{0,2},{1,3},{2,4},{3,5},{4,6},{5,7},{6,0},{7,1},{8,10},{9,11},{10,... | collective-permute-start | bytes 1179656 | tf_op jit(solution)/shard_map/ppermute | solution.py:36
  90.6 19.4 %collective-permute-start.13 = (bf16[8,48,512]{2,1,0:T(8,128)(2,1)}, bf16[8,48,512]{2,1,0:T(8,128)(2,1)}, u32[]{:S(2)}, u32[]{:S(2)}) collective-permute-start(bf16[8,48,512]{2,1,0:T(8,128)(2,1)} %add_convert_fusion.4), channel_id=1, source_target_pairs={{0,1},{1,0},{2,3},{3,2},{4,5},{5,4},{6,7},{7,6},{8,9},{9,8},{10,11... | collective-permute-start | bytes 1179656 | tf_op jit(solution)/shard_map/ppermute | solution.py:42
  94.0 31.5 %collective-permute-start.18 = (bf16[8,48,512]{2,1,0:T(8,128)(2,1)}, bf16[8,48,512]{2,1,0:T(8,128)(2,1)S(1)}, u32[]{:S(2)}, u32[]{:S(2)}) collective-permute-start(bf16[8,48,512]{2,1,0:T(8,128)(2,1)} %add_convert_fusion.1), channel_id=1, source_target_pairs={{0,1},{1,0},{2,3},{3,2},{4,5},{5,4},{6,7},{7,6},{8,9},{9,8},{10,11... | collective-permute-start | bytes 1179656 | tf_op jit(solution)/shard_map/ppermute | solution.py:42
  99.8 2.1 %collective-permute-start.10 = (bf16[8,96,128]{2,1,0:T(8,128)(2,1)S(1)}, bf16[8,96,128]{2,1,0:T(8,128)(2,1)S(1)}, u32[]{:S(2)}, u32[]{:S(2)}) collective-permute-start(bf16[8,96,128]{2,1,0:T(8,128)(2,1)S(1)} %slice.28.own_ref), channel_id=1, source_target_pairs={{0,64},{64,0},{1,65},{65,1},{2,66},{66,2},{3,67},{67,3},{4,68},{68... | collective-permute-start | bytes 589832 | tf_op jit(solution)/shard_map/ppermute | solution.py:342
  106.3 19.2 %copy-start.6 = (bf16[8,48,512]{2,1,0:T(8,128)(2,1)S(1)}, bf16[8,48,512]{2,1,0:T(8,128)(2,1)}, u32[]{:S(2)}) copy-start(bf16[8,48,512]{2,1,0:T(8,128)(2,1)} %get-tuple-element.55.after_ref) | copy-start | bytes 1179652
  106.3 17.5 %all-to-all-start.3 = ((bf16[8,352,128]{2,1,0:T(8,128)(2,1)}), bf16[8,352,128]{2,1,0:T(8,128)(2,1)S(1)}, u32[]{:S(2)}, u32[]{:S(2)}) async-start(bf16[8,352,128]{2,1,0:T(8,128)(2,1)} %pad_maximum_fusion.2), calls=%async_computation.3 | async-start | bytes 1441792 | tf_op jit(solution)/shard_map/all_to_all | solution.py:346
  111.3 14.2 %collective-permute-start.15 = (bf16[8,48,512]{2,1,0:T(8,128)(2,1)S(1)}, bf16[8,48,512]{2,1,0:T(8,128)(2,1)}, u32[]{:S(2)}, u32[]{:S(2)}) collective-permute-start(bf16[8,48,512]{2,1,0:T(8,128)(2,1)S(1)} %add_convert_fusion.3), channel_id=1, source_target_pairs={{0,2},{1,3},{2,4},{3,5},{4,6},{5,7},{6,0},{7,1},{8,10},{9,11},{10,... | collective-permute-start | bytes 1179656 | tf_op jit(solution)/shard_map/ppermute | solution.py:36
  124.6 4.6 %collective-permute-start.19 = (bf16[2048,128]{1,0:T(8,128)(2,1)}, bf16[2048,128]{1,0:T(8,128)(2,1)}, u32[]{:S(2)}, u32[]{:S(2)}) collective-permute-start(bf16[2048,128]{1,0:T(8,128)(2,1)} %bitcast.21), channel_id=1, source_target_pairs={{0,64},{64,0},{1,65},{65,1},{2,66},{66,2},{3,67},{67,3},{4,68},{68... | collective-permute-start | bytes 1572872 | tf_op jit(solution)/shard_map/ppermute | solution.py:342
  (16 other events, 79.0 us)
where the time goes:
time: 133 us; the launch traced here: 132 us
  starting transfers between devices  45.1 us (34%)
  Pallas kernels  31.5 us (24%)
  waiting for transfers between devices  23.1 us (17%)
  other arithmetic  16.7 us (13%)
  local copies, waits for them, and re-layouts  13.9 us (10%)
  between operations  1.72 us (1%)
    all_to_all x4, waiting for transfers between devices, exchange(): return lax.all_to_all(x, 'dp', 0, 0, tiled=True)  22 us
    all_to_all x4, starting transfers between devices, exchange(): return lax.all_to_all(x, 'dp', 0, 0, tiled=True)  20.1 us
    ppermute x6, starting transfers between devices, down(): return lax.ppermute(x, self.name, self.perm_down)  10.6 us
    pallas_call x1, Pallas kernels, kernel_grad(): pl.pallas_call(kernel_grad_kernel, out_shape=[jax.ShapeDtypeStruct((2048,...  10.5 us
    pallas_call x1, Pallas kernels, forward(): pl.pallas_call(forward_kernel, out_shape=[jax.ShapeDtypeStruct((rows, wid...  9.29 us
    pallas_call x1, Pallas kernels, input_partials(): pl.pallas_call(input_grad_kernel, out_shape=[whole] * 7 + [half] * 2, in_...  8.14 us
    ppermute x4, starting transfers between devices, core_swap(): return lax.ppermute(x, 'rep', [(0, 1), (1, 0)])  5.82 us
    convert_element_type x4, other arithmetic, added(): return sum((x.astype(F32) for x in terms)).astype(BF16)  5.66 us
  transfers between devices with their start and end apart: 24, of which 4 were waited for; matrix products, arithmetic and copies ran while one was open for 15% of the time, Pallas kernels for 16%

commit v1 on v0

--- a/solution.py
+++ b/solution.py
@@ -354,22 +354,16 @@
     return pick(row, origin, own, core_swap(own))
 
 
-def first_exchange(mine, theirs, payload):
-    pair = (mine + core_swap(theirs)).astype(BF16).reshape(8, 256, 128)
-    return jnp.concatenate([pair, payload], 1)
-
-
-def second_exchange(spread, scale, source):
+def chip_sum(mine, theirs):
+    return (mine + core_swap(theirs)).astype(BF16).reshape(8, 256, 128)
+
+
+def both_cores(half):
     rep = lax.axis_index("rep")
-    handed = handed_on(spread[:, 256:], source)
-    share = (jnp.sum(spread[:, :256].astype(F32), 0) * scale).astype(BF16)
-    share = jnp.broadcast_to(share[None], (8, 256, 128))
-    spread = exchange(jnp.concatenate([share, handed], 1))
-    half = spread[:, :256].reshape(2048, 128)
     there = core_swap(half)
     low = jnp.where(rep == 0, half, there)
     high = jnp.where(rep == 0, there, half)
-    return jnp.concatenate([low, high], 0), spread[:, 256:]
+    return jnp.concatenate([low, high], 0)
 
 
 def per_device(frames, weight, cotangent, prev_owner, lengths):
@@ -390,22 +384,26 @@
     payload, x = lax.optimization_barrier((m[:, :, :256], x))
     payload = exchange(payload)
     blocks = tensor.gather(x)
+    payload, _ = lax.optimization_barrier((payload, (blocks[1], blocks[2])))
     head = exchange(handed_on(payload, follower))
     keep = jnp.arange(seg_len) < lengths[member]
     keep_head = jnp.arange(2) < lengths[jnp.maximum(follower[member], 0)]
     live = jnp.concatenate([keep, keep_head]).astype(jnp.int32)
 
     partials = input_partials(place, live, m, head, rows)
-    partials, blocks = lax.optimization_barrier((partials, blocks))
     mine, theirs = kernel_grad(place, live, rep.astype(jnp.int32)[None], partials[0], blocks, m, head)
-    conv, carry = forward(place, theirs, blocks, rows)
-    spread = first_exchange(mine, theirs, carry)
+    spread = chip_sum(mine, theirs)
+    partials, spread = lax.optimization_barrier((partials, spread))
+    conv, carry = forward(place, spread, blocks, rows)
+    conv = conv.reshape(height, width, seg_len, columns).transpose(2, 1, 0, 3)
     input_grad = from_rows(tensor.scatter_sum(partials))
 
     cells = prev_owner.shape[0] * seg_len * height * columns
-    conv = conv.reshape(height, width, seg_len, columns).transpose(2, 1, 0, 3)
-    spread, conv = lax.optimization_barrier((exchange(spread), conv))
-    total, received = second_exchange(spread, 1.0 / math.sqrt(cells), prev_owner)
+    share = (jnp.sum(exchange(spread).astype(F32), 0) * (1.0 / math.sqrt(cells))).astype(BF16)
+    share = jnp.broadcast_to(share[None], spread.shape)
+    spread, conv = lax.optimization_barrier((exchange(jnp.concatenate([share, carry], 1)), conv))
+    received = exchange(handed_on(spread[:, 256:], prev_owner))
+    total = both_cores(spread[:, :256].reshape(2048, 128))
     total = total[: 81 * width].reshape(3, 3, 3, 3, width, 128)
     weight_grad = total[:, :, ::-1].transpose(4, 0, 2, 3, 1, 5).reshape(weight.shape).astype(F32)
 

time: 133 us -> 135 us (1.015)
  starting transfers between devices: 45.1 us -> 52.9 us
  waiting for transfers between devices: 23.1 us -> 20.2 us
  local copies, waits for them, and re-layouts: 13.9 us -> 11.7 us
    all_to_all x4 -> x5, starting transfers between devices: 20.1 us -> 27.2 us  [exchange(): return lax.all_to_all(x, 'dp', 0, 0, tiled=True)]
    all_to_all x4 -> x5, waiting for transfers between devices: 22 us -> 15.1 us  [exchange(): return lax.all_to_all(x, 'dp', 0, 0, tiled=True)]
    ppermute x6, starting transfers between devices: 10.6 us -> 16 us  [down(): return lax.ppermute(x, self.name, self.perm_down)]
    ppermute x6, starting transfers between devices: 4.89 us -> 0.27 us  [up(): return lax.ppermute(x, self.name, self.perm_up)]
    ppermute x6, waiting for transfers between devices: 0.02 us -> 2.22 us  [up(): return lax.ppermute(x, self.name, self.perm_up)]
    convert_element_type x2, other arithmetic: 0.11 us -> 2.22 us  [the longest x1 2.21 us: chip_sum(): return (mine + core_swap(theirs)).astype(BF16).reshape(8, 256, 128)]
    concatenate x3 -> x2, other arithmetic: 2.81 us -> 0.97 us  [the longest x1 0.91 us: per_device(): jnp.concatenate([share, carry], 1)]
    ppermute x4, waiting for transfers between devices: 1.07 us -> 2.77 us  [core_swap(): return lax.ppermute(x, 'rep', [(0, 1), (1, 0)])]
  transfers between devices with their start and end apart: 24 -> 25, of which waited for: 4 -> 7; matrix products, arithmetic and copies ran while one was open for 15% -> 12% of each run, Pallas kernels for 16% -> 16%
where the time goes in v1:
time: 135 us; the launch traced here: 134 us
  starting transfers between devices  52.9 us (39%)
  Pallas kernels  31.4 us (23%)
  waiting for transfers between devices  20.2 us (15%)
  other arithmetic  15.8 us (12%)
  local copies, waits for them, and re-layouts  11.7 us (9%)
  between operations  1.76 us (1%)
    all_to_all x5, starting transfers between devices, exchange(): return lax.all_to_all(x, 'dp', 0, 0, tiled=True)  27.2 us
    ppermute x6, starting transfers between devices, down(): return lax.ppermute(x, self.name, self.perm_down)  16 us
    all_to_all x5, waiting for transfers between devices, exchange(): return lax.all_to_all(x, 'dp', 0, 0, tiled=True)  15.1 us
    pallas_call x1, Pallas kernels, kernel_grad(): pl.pallas_call(kernel_grad_kernel, out_shape=[jax.ShapeDtypeStruct((2048,...  10.4 us
    pallas_call x1, Pallas kernels, forward(): pl.pallas_call(forward_kernel, out_shape=[jax.ShapeDtypeStruct((rows, wid...  9.29 us
    pallas_call x1, Pallas kernels, input_partials(): pl.pallas_call(input_grad_kernel, out_shape=[whole] * 7 + [half] * 2, in_...  8.11 us
    ppermute x4, starting transfers between devices, core_swap(): return lax.ppermute(x, 'rep', [(0, 1), (1, 0)])  6.35 us
    convert_element_type x4, other arithmetic, added(): return sum((x.astype(F32) for x in terms)).astype(BF16)  4.37 us
  transfers between devices with their start and end apart: 25, of which 7 were waited for; matrix products, arithmetic and copies ran while one was open for 12% of the time, Pallas kernels for 16%

profile of v1, /device:TPU:1, one launch (start us, length us, event | category | flops | bytes accessed | tf_op | source)
XLA Modules:
  0.0 133.7 jit_solution(15304499228007574921)
XLA Ops:
  0.7 1.3 %copy.25 = bf16[8,48,4,128]{3,2,1,0:T(4,128)(2,1)S(1)} copy(bf16[8,48,4,128]{3,0,1,2:T(8,128)(2,1)} %bitcast.46) | data formatting | bytes 786432 | tf_op jit(solution)/shard_map/transpose | solution.py:333
  3.4 4.7 %collective-permute-start = (bf16[8,48,512]{2,1,0:T(8,128)(2,1)S(1)}, bf16[8,48,512]{2,1,0:T(8,128)(2,1)S(1)}, u32[]{:S(2)}, u32[]{:S(2)}) collective-permute-start(bf16[8,48,512]{2,1,0:T(8,128)(2,1)S(1)} %reshape.48.rest_0_), channel_id=1, source_target_pairs={{0,6},{1,7},{2,0},{3,1},{4,2},{5,3},{6,4},{7,5},{8,14},{9,15},{10,... | collective-permute-start | bytes 1179656 | tf_op jit(solution)/shard_map/ppermute | solution.py:39
  8.0 1.3 collective-permute-start.2
  9.3 6.4 %all-to-all-start = ((bf16[8,48,256]{2,1,0:T(8,128)(2,1)}), bf16[8,48,256]{2,1,0:T(8,128)(2,1)S(1)}, u32[]{:S(2)}, u32[]{:S(2)}) async-start(bf16[8,48,256]{2,1,0:T(8,128)(2,1)} %slice.24), calls=%async_computation | async-start | bytes 393216 | tf_op jit(solution)/shard_map/all_to_all | solution.py:346
  17.7 1.2 collective-permute-done.1.rest_3_
  19.7 1.3 collective-permute-start.4
  21.0 2.0 %all-to-all-done.own_ref = bf16[8,48,256]{2,1,0:T(8,128)(2,1)S(1)} async-done(((bf16[8,48,256]{2,1,0:T(8,128)(2,1)}), bf16[8,48,256]{2,1,0:T(8,128)(2,1)S(1)}, u32[]{:S(2)}, u32[]{:S(2)}) %all-to-all-start) | async-done | bytes 196640 | tf_op jit(solution)/shard_map/all_to_all | solution.py:346
  23.0 2.7 %collective-permute-start.3 = (bf16[8,48,256]{2,1,0:T(8,128)(2,1)S(1)}, bf16[8,48,256]{2,1,0:T(8,128)(2,1)S(1)}, u32[]{:S(2)}, u32[]{:S(2)}) collective-permute-start(bf16[8,48,256]{2,1,0:T(8,128)(2,1)S(1)} %all-to-all-done.own_ref), channel_id=1, source_target_pairs={{0,64},{64,0},{1,65},{65,1},{2,66},{66,2},{3,67},{67,3},{4,68},{68... | collective-permute-start | bytes 589832 | tf_op jit(solution)/shard_map/ppermute | solution.py:342
  27.8 1.7 %pick.2 = bf16[8,48,256]{2,1,0:T(8,128)(2,1)} custom-call(s32[8]{0:T(128)} %get-tuple-element.70.row_ref, s32[8]{0:T(128)} %get-tuple-element.69.from_ref, bf16[8,48,256]{2,1,0:T(8,128)(2,1)} %copy-done.3, bf16[8,48,256]{2,1,0:T(8,128)(2,1)} %copy-done.13), custom_call_target="tpu_custom_call" | custom-call | tf_op jit(solution)/shard_map/pick/pallas_call | solution.py:278
  29.5 3.8 %all-to-all-start.1 = ((bf16[8,48,256]{2,1,0:T(8,128)(2,1)}), bf16[8,48,256]{2,1,0:T(8,128)(2,1)S(1)}, u32[]{:S(2)}, u32[]{:S(2)}) async-start(bf16[8,48,256]{2,1,0:T(8,128)(2,1)} %pick.2), calls=%async_computation.1 | async-start | bytes 393216 | tf_op jit(solution)/shard_map/all_to_all | solution.py:346
  34.0 2.9 %collective-permute-start.6 = (bf16[8,48,512]{2,1,0:T(8,128)(2,1)S(1)}, bf16[8,48,512]{2,1,0:T(8,128)(2,1)}, u32[]{:S(2)}, u32[]{:S(2)}) collective-permute-start(bf16[8,48,512]{2,1,0:T(8,128)(2,1)S(1)} %collective-permute-done.rest_2_), channel_id=1, source_target_pairs={{0,6},{1,7},{2,0},{3,1},{4,2},{5,3},{6,4},{7,5},{8,14},{9,15},{10,... | collective-permute-start | bytes 1179656 | tf_op jit(solution)/shard_map/ppermute | solution.py:39
  39.2 1.5 %collective-permute-start.7 = (bf16[4,48,512]{2,1,0:T(8,128)(2,1)S(1)}, bf16[4,48,512]{2,1,0:T(8,128)(2,1)S(1)}, u32[]{:S(2)}, u32[]{:S(2)}) collective-permute-start(bf16[4,48,512]{2,1,0:T(8,128)(2,1)S(1)} %slice.25), channel_id=1, source_target_pairs={{0,6},{1,7},{2,0},{3,1},{4,2},{5,3},{6,4},{7,5},{8,14},{9,15},{10,... | collective-permute-start | bytes 589832 | tf_op jit(solution)/shard_map/ppermute | solution.py:39
  41.7 8.1 %input_partials.1 = (bf16[8,48,512]{2,1,0:T(8,128)(2,1)}, bf16[8,48,512]{2,1,0:T(8,128)(2,1)}, bf16[8,48,512]{2,1,0:T(8,128)(2,1)}, bf16[8,48,512]{2,1,0:T(8,128...) custom-call(s32[8]{0:T(128)} %stack.35.place_ref, ...), custom_call_target="tpu_custom_call" | custom-call | flops 4076863488 | bytes 5000000 | tf_op jit(solution)/shard_map/input_partials/pallas_call | solution.py:260
  50.7 10.4 %kernel_grad.1 = (f32[2048,128]{1,0:T(8,128)}, f32[2048,128]{1,0:T(8,128)}) custom-call(s32[8]{0:T(128)} %stack.35.place_ref, s32[6]{0:T(128)} %add_convert_fusion.5.live_ref, s32[1]{0:T(128)} %bitcast.15.rep_ref, bf16[8,48,512]{2,1,0:T(8,128)(2,1)} %get-tuple-element.56.after_ref, bf16[8,48,512]{2,1,0:T(8,128)(2,1)} %copy-done.7, ...), custom_call_target="tpu_custom_call" | custom-call | flops 4076863488 | bytes 6000000 | tf_op jit(solution)/shard_map/kernel_grad/pallas_call | solution.py:312
  61.1 1.4 %collective-permute-start.9 = (f32[2048,128]{1,0:T(8,128)}, f32[2048,128]{1,0:T(8,128)S(1)}, u32[]{:S(2)}, u32[]{:S(2)}) collective-permute-start(f32[2048,128]{1,0:T(8,128)} %get-tuple-element.50), channel_id=1, source_target_pairs={{0,64},{64,0},{1,65},{65,1},{2,66},{66,2},{3,67},{67,3},{4,68},{68... | collective-permute-start | bytes 3145736 | tf_op jit(solution)/shard_map/ppermute | solution.py:342
  62.5 2.5 %collective-permute-done.9 = f32[2048,128]{1,0:T(8,128)S(1)} collective-permute-done((f32[2048,128]{1,0:T(8,128)}, f32[2048,128]{1,0:T(8,128)S(1)}, u32[]{:S(2)}, u32[]{:S(2)}) %collective-permute-start.9) | collective-permute-done | bytes 1048608 | tf_op jit(solution)/shard_map/ppermute | solution.py:342
  65.0 2.2 %add_convert_fusion = bf16[2048,128]{1,0:T(8,128)(2,1)} fusion(f32[2048,128]{1,0:T(8,128)} %get-tuple-element.49, f32[2048,128]{1,0:T(8,128)S(1)} %collective-permute-done.9), kind=kLoop, calls=%fused_computation.3 | loop fusion | flops 524288 | bytes 2621440 | tf_op jit(solution)/shard_map/convert_element_type | solution.py:358
  67.2 6.8 %all-to-all-start.2 = ((bf16[8,256,128]{2,1,0:T(8,128)(2,1)}), bf16[8,256,128]{2,1,0:T(8,128)(2,1)S(1)}, u32[]{:S(2)}, u32[]{:S(2)}) async-start(bf16[8,256,128]{2,1,0:T(8,128)(2,1)} %bitcast.16.after_ref), calls=%async_computation.2 | async-start | bytes 1048576 | tf_op jit(solution)/shard_map/all_to_all | solution.py:346
  74.0 2.7 %collective-permute-start.16 = (bf16[4,48,512]{2,1,0:T(8,128)(2,1)S(1)}, bf16[4,48,512]{2,1,0:T(8,128)(2,1)S(1)}, u32[]{:S(2)}, u32[]{:S(2)}) collective-permute-start(bf16[4,48,512]{2,1,0:T(8,128)(2,1)S(1)} %copy-done.26), channel_id=1, source_target_pairs={{0,6},{1,7},{2,0},{3,1},{4,2},{5,3},{6,4},{7,5},{8,14},{9,15},{10,... | collective-permute-start | bytes 589832 | tf_op jit(solution)/shard_map/ppermute | solution.py:39
  76.8 2.7 %collective-permute-start.11 = (bf16[8,48,512]{2,1,0:T(8,128)(2,1)}, bf16[8,48,512]{2,1,0:T(8,128)(2,1)}, u32[]{:S(2)}, u32[]{:S(2)}) collective-permute-start(bf16[8,48,512]{2,1,0:T(8,128)(2,1)} %get-tuple-element.57), channel_id=1, source_target_pairs={{0,6},{1,7},{2,0},{3,1},{4,2},{5,3},{6,4},{7,5},{8,14},{9,15},{10,... | collective-permute-start | bytes 1179656 | tf_op jit(solution)/shard_map/ppermute | solution.py:39
  79.5 9.3 %forward.1 = (f32[8,48,512]{2,1,0:T(8,128)}, bf16[8,96,128]{2,1,0:T(8,128)(2,1)}) custom-call(s32[8]{0:T(128)} %stack.35.place_ref, bf16[8,256,128]{2,1,0:T(8,128)(2,1)} %bitcast.16.after_ref, bf16[8,48,512]{2,1,0:T(8,128)(2,1)} %copy-done.7, bf16[8,48,512]{2,1,0:T(8,128)(2,1)} %collective-permute-done.2.rest_1_, bf16[8,48,512]{2,1,0:T(8,128)(2,1)} %copy-done.21, ...), custom_call_target="tpu_custom_call" | custom-call | flops 4076863488 | bytes 5000000 | tf_op jit(solution)/shard_map/forward/pallas_call | solution.py:291
  89.6 1.4 %collective-permute-start.17 = (bf16[8,48,512]{2,1,0:T(8,128)(2,1)}, bf16[8,48,512]{2,1,0:T(8,128)(2,1)}, u32[]{:S(2)}, u32[]{:S(2)}) collective-permute-start(bf16[8,48,512]{2,1,0:T(8,128)(2,1)} %add_convert_fusion.2), channel_id=1, source_target_pairs={{0,6},{1,7},{2,0},{3,1},{4,2},{5,3},{6,4},{7,5},{8,14},{9,15},{10,... | collective-permute-start | bytes 1179656 | tf_op jit(solution)/shard_map/ppermute | solution.py:39
  94.0 6.8 %all-to-all-start.3 = ((bf16[8,352,128]{2,1,0:T(8,128)(2,1)}), bf16[8,352,128]{2,1,0:T(8,128)(2,1)S(1)}, u32[]{:S(2)}, u32[]{:S(2)}) async-start(bf16[8,352,128]{2,1,0:T(8,128)(2,1)} %pad_maximum_fusion.1), calls=%async_computation.3 | async-start | bytes 1441792 | tf_op jit(solution)/shard_map/all_to_all | solution.py:346
  100.9 1.8 %add_convert_fusion.1 = bf16[8,48,512]{2,1,0:T(8,128)(2,1)} fusion(bf16[8,48,512]{2,1,0:T(8,128)(2,1)} %collective-permute-done.17, bf16[8,48,512]{2,1,0:T(8,128)(2,1)S(1)} %copy-done.9), kind=kLoop, calls=%fused_computation.8 | loop fusion | flops 786432 | bytes 1179648 | tf_op jit(solution)/shard_map/convert_element_type | solution.py:73
  104.9 8.7 %all-to-all-done.3 = bf16[8,352,128]{2,1,0:T(8,128)(2,1)S(1)} async-done(((bf16[8,352,128]{2,1,0:T(8,128)(2,1)}), bf16[8,352,128]{2,1,0:T(8,128)(2,1)S(1)}, u32[]{:S(2)}, u32[]{:S(2)}) %all-to-all-start.3) | async-done | bytes 720928 | tf_op jit(solution)/shard_map/all_to_all | solution.py:346
  113.6 2.1 %collective-permute-start.10 = (bf16[8,96,128]{2,1,0:T(8,128)(2,1)S(1)}, bf16[8,96,128]{2,1,0:T(8,128)(2,1)S(1)}, u32[]{:S(2)}, u32[]{:S(2)}) collective-permute-start(bf16[8,96,128]{2,1,0:T(8,128)(2,1)S(1)} %slice.21.own_ref), channel_id=1, source_target_pairs={{0,64},{64,0},{1,65},{65,1},{2,66},{66,2},{3,67},{67,3},{4,68},{68... | collective-permute-start | bytes 589832 | tf_op jit(solution)/shard_map/ppermute | solution.py:342
  117.5 1.8 %pick.3 = bf16[8,96,128]{2,1,0:T(8,128)(2,1)} custom-call(s32[8]{0:T(128)} %get-tuple-element.68.row_ref, s32[8]{0:T(128)} %get-tuple-element.67.from_ref, bf16[8,96,128]{2,1,0:T(8,128)(2,1)} %copy-done.4, bf16[8,96,128]{2,1,0:T(8,128)(2,1)} %copy-done.14), custom_call_target="tpu_custom_call" | custom-call | tf_op jit(solution)/shard_map/pick/pallas_call | solution.py:278
  119.3 3.4 %all-to-all-start.4 = ((bf16[8,96,128]{2,1,0:T(8,128)(2,1)}), bf16[8,96,128]{2,1,0:T(8,128)(2,1)S(1)}, u32[]{:S(2)}, u32[]{:S(2)}) async-start(bf16[8,96,128]{2,1,0:T(8,128)(2,1)} %pick.3), calls=%async_computation.4 | async-start | bytes 393216 | tf_op jit(solution)/shard_map/all_to_all | solution.py:346
  122.7 1.4 %convert_add_fusion = f32[8,48,512]{2,1,0:T(8,128)S(1)} fusion(bf16[8,48,512]{2,1,0:T(8,128)(2,1)} %collective-permute-done.18, bf16[8,48,512]{2,1,0:T(8,128)(2,1)} %collective-permute-done.15, bf16[8,48,512]{2,1,0:T(8,128)(2,1)} %collective-permute-done.11, bf16[8,48,512]{2,1,0:T(8,128)(2,1)S(1)} %copy-done.5), kind=kLoop, calls=%fused_computation.7 | loop fusion | flops 1376256 | bytes 2359296 | tf_op jit(solution)/shard_map/add | solution.py:69
  124.4 1.3 %copy.36 = f32[8,48,4,128]{3,0,1,2:T(8,128)} copy(f32[8,48,4,128]{3,2,1,0:T(4,128)S(1)} %reshape.52) | data formatting | bytes 1572864 | tf_op jit(solution)/shard_map/reshape | solution.py:338
  125.7 4.4 %all-to-all-done.4 = bf16[8,96,128]{2,1,0:T(8,128)(2,1)S(1)} async-done(((bf16[8,96,128]{2,1,0:T(8,128)(2,1)}), bf16[8,96,128]{2,1,0:T(8,128)(2,1)S(1)}, u32[]{:S(2)}, u32[]{:S(2)}) %all-to-all-start.4) | async-done | bytes 196640 | tf_op jit(solution)/shard_map/all_to_all | solution.py:346
  132.3 1.4 %copy_bitcast_fusion = f32[48,3,3,3,384]{4,0,3,2,1:T(8,128)} fusion(bf16[3,3,3,3,48,128]{5,4,3,2,1,0:T(8,128)(2,1)S(1)} %bitcast.37), kind=kLoop, calls=%fused_computation | loop fusion | flops 497664 | bytes 2985984 | tf_op jit(solution)/shard_map/convert_element_type | solution.py:408
  (115 shorter events, 20.2 us)
Async XLA Ops:
  0.7 16.4 %copy-start.18 = (s32[16]{0:T(128)S(1)}, s32[16]{0:T(128)}, u32[]{:S(2)}) copy-start(s32[16]{0:T(128)} %param.9) | copy-start | bytes 196
  2.0 35.5 %copy-start = (bf16[48,3,3,3,384]{4,0,3,2,1:T(8,128)(2,1)S(1)}, bf16[48,3,3,3,384]{4,0,3,2,1:T(8,128)(2,1)}, u32[]{:S(2)}) copy-start(bf16[48,3,3,3,384]{4,0,3,2,1:T(8,128)(2,1)} %param.6) | copy-start | bytes 2985988
  2.2 36.4 %copy-start.1 = (bf16[8,48,512]{2,1,0:T(8,128)(2,1)}, bf16[8,48,512]{2,1,0:T(8,128)(2,1)S(1)}, u32[]{:S(2)}) copy-start(bf16[8,48,512]{2,1,0:T(8,128)(2,1)S(1)} %reshape.47.m_ref.rest_9_) | copy-start | bytes 1179652
  3.4 35.9 %copy-start.7 = (bf16[8,48,512]{2,1,0:T(8,128)(2,1)}, bf16[8,48,512]{2,1,0:T(8,128)(2,1)S(1)}, u32[]{:S(2)}) copy-start(bf16[8,48,512]{2,1,0:T(8,128)(2,1)S(1)} %reshape.48.rest_0_) | copy-start | bytes 1179652
  3.4 14.3 %collective-permute-start = (bf16[8,48,512]{2,1,0:T(8,128)(2,1)S(1)}, bf16[8,48,512]{2,1,0:T(8,128)(2,1)S(1)}, u32[]{:S(2)}, u32[]{:S(2)}) collective-permute-start(bf16[8,48,512]{2,1,0:T(8,128)(2,1)S(1)} %reshape.48.rest_0_), channel_id=1, source_target_pairs={{0,6},{1,7},{2,0},{3,1},{4,2},{5,3},{6,4},{7,5},{8,14},{9,15},{10,... | collective-permute-start | bytes 1179656 | tf_op jit(solution)/shard_map/ppermute | solution.py:39
  8.0 10.9 %collective-permute-start.1 = (bf16[8,48,512]{2,1,0:T(8,128)(2,1)S(1)}, bf16[8,48,512]{2,1,0:T(8,128)(2,1)S(1)}, u32[]{:S(2)}, u32[]{:S(2)}) collective-permute-start(bf16[8,48,512]{2,1,0:T(8,128)(2,1)S(1)} %reshape.48.rest_0_), channel_id=1, source_target_pairs={{0,2},{1,3},{2,4},{3,5},{4,6},{5,7},{6,0},{7,1},{8,10},{9,11},{10,... | collective-permute-start | bytes 1179656 | tf_op jit(solution)/shard_map/ppermute | solution.py:36
  8.0 11.6 %collective-permute-start.2 = (bf16[8,48,512]{2,1,0:T(8,128)(2,1)S(1)}, bf16[8,48,512]{2,1,0:T(8,128)(2,1)}, u32[]{:S(2)}, u32[]{:S(2)}) collective-permute-start(bf16[8,48,512]{2,1,0:T(8,128)(2,1)S(1)} %reshape.48.rest_0_), channel_id=1, source_target_pairs={{0,1},{1,0},{2,3},{3,2},{4,5},{5,4},{6,7},{7,6},{8,9},{9,8},{10,11... | collective-permute-start | bytes 1179656 | tf_op jit(solution)/shard_map/ppermute | solution.py:42
  9.3 13.7 %all-to-all-start = ((bf16[8,48,256]{2,1,0:T(8,128)(2,1)}), bf16[8,48,256]{2,1,0:T(8,128)(2,1)S(1)}, u32[]{:S(2)}, u32[]{:S(2)}) async-start(bf16[8,48,256]{2,1,0:T(8,128)(2,1)} %slice.24), calls=%async_computation | async-start | bytes 393216 | tf_op jit(solution)/shard_map/all_to_all | solution.py:346
  17.7 32.1 %copy-start.21 = (bf16[8,48,512]{2,1,0:T(8,128)(2,1)}, bf16[8,48,512]{2,1,0:T(8,128)(2,1)S(1)}, u32[]{:S(2)}) copy-start(bf16[8,48,512]{2,1,0:T(8,128)(2,1)S(1)} %collective-permute-done.rest_2_) | copy-start | bytes 1179652
  19.7 19.5 %collective-permute-start.4 = (bf16[8,48,512]{2,1,0:T(8,128)(2,1)S(1)}, bf16[8,48,512]{2,1,0:T(8,128)(2,1)S(1)}, u32[]{:S(2)}, u32[]{:S(2)}) collective-permute-start(bf16[8,48,512]{2,1,0:T(8,128)(2,1)S(1)} %collective-permute-done.rest_2_), channel_id=1, source_target_pairs={{0,1},{1,0},{2,3},{3,2},{4,5},{5,4},{6,7},{7,6},{8,9},{9,8},{10,11... | collective-permute-start | bytes 1179656 | tf_op jit(solution)/shard_map/ppermute | solution.py:42
  20.9 19.8 %collective-permute-start.5 = (bf16[8,48,512]{2,1,0:T(8,128)(2,1)}, bf16[8,48,512]{2,1,0:T(8,128)(2,1)S(1)}, u32[]{:S(2)}, u32[]{:S(2)}) collective-permute-start(bf16[8,48,512]{2,1,0:T(8,128)(2,1)} %collective-permute-done.2.rest_1_), channel_id=1, source_target_pairs={{0,2},{1,3},{2,4},{3,5},{4,6},{5,7},{6,0},{7,1},{8,10},{9,11},{10,... | collective-permute-start | bytes 1179656 | tf_op jit(solution)/shard_map/ppermute | solution.py:36
  23.0 4.1 %collective-permute-start.3 = (bf16[8,48,256]{2,1,0:T(8,128)(2,1)S(1)}, bf16[8,48,256]{2,1,0:T(8,128)(2,1)S(1)}, u32[]{:S(2)}, u32[]{:S(2)}) collective-permute-start(bf16[8,48,256]{2,1,0:T(8,128)(2,1)S(1)} %all-to-all-done.own_ref), channel_id=1, source_target_pairs={{0,64},{64,0},{1,65},{65,1},{2,66},{66,2},{3,67},{67,3},{4,68},{68... | collective-permute-start | bytes 589832 | tf_op jit(solution)/shard_map/ppermute | solution.py:342
  29.5 11.5 %all-to-all-start.1 = ((bf16[8,48,256]{2,1,0:T(8,128)(2,1)}), bf16[8,48,256]{2,1,0:T(8,128)(2,1)S(1)}, u32[]{:S(2)}, u32[]{:S(2)}) async-start(bf16[8,48,256]{2,1,0:T(8,128)(2,1)} %pick.2), calls=%async_computation.1 | async-start | bytes 393216 | tf_op jit(solution)/shard_map/all_to_all | solution.py:346
  34.0 15.9 %collective-permute-start.6 = (bf16[8,48,512]{2,1,0:T(8,128)(2,1)S(1)}, bf16[8,48,512]{2,1,0:T(8,128)(2,1)}, u32[]{:S(2)}, u32[]{:S(2)}) collective-permute-start(bf16[8,48,512]{2,1,0:T(8,128)(2,1)S(1)} %collective-permute-done.rest_2_), channel_id=1, source_target_pairs={{0,6},{1,7},{2,0},{3,1},{4,2},{5,3},{6,4},{7,5},{8,14},{9,15},{10,... | collective-permute-start | bytes 1179656 | tf_op jit(solution)/shard_map/ppermute | solution.py:39
  39.2 10.7 %collective-permute-start.7 = (bf16[4,48,512]{2,1,0:T(8,128)(2,1)S(1)}, bf16[4,48,512]{2,1,0:T(8,128)(2,1)S(1)}, u32[]{:S(2)}, u32[]{:S(2)}) collective-permute-start(bf16[4,48,512]{2,1,0:T(8,128)(2,1)S(1)} %slice.25), channel_id=1, source_target_pairs={{0,6},{1,7},{2,0},{3,1},{4,2},{5,3},{6,4},{7,5},{8,14},{9,15},{10,... | collective-permute-start | bytes 589832 | tf_op jit(solution)/shard_map/ppermute | solution.py:39
  40.8 9.1 %collective-permute-start.8 = (bf16[4,48,512]{2,1,0:T(8,128)(2,1)S(1)}, bf16[4,48,512]{2,1,0:T(8,128)(2,1)S(1)}, u32[]{:S(2)}, u32[]{:S(2)}) collective-permute-start(bf16[4,48,512]{2,1,0:T(8,128)(2,1)S(1)} %slice.26), channel_id=1, source_target_pairs={{0,2},{1,3},{2,4},{3,5},{4,6},{5,7},{6,0},{7,1},{8,10},{9,11},{10,... | collective-permute-start | bytes 589832 | tf_op jit(solution)/shard_map/ppermute | solution.py:36
  61.1 3.9 %collective-permute-start.9 = (f32[2048,128]{1,0:T(8,128)}, f32[2048,128]{1,0:T(8,128)S(1)}, u32[]{:S(2)}, u32[]{:S(2)}) collective-permute-start(f32[2048,128]{1,0:T(8,128)} %get-tuple-element.50), channel_id=1, source_target_pairs={{0,64},{64,0},{1,65},{65,1},{2,66},{66,2},{3,67},{67,3},{4,68},{68... | collective-permute-start | bytes 3145736 | tf_op jit(solution)/shard_map/ppermute | solution.py:342
  67.2 25.7 %all-to-all-start.2 = ((bf16[8,256,128]{2,1,0:T(8,128)(2,1)}), bf16[8,256,128]{2,1,0:T(8,128)(2,1)S(1)}, u32[]{:S(2)}, u32[]{:S(2)}) async-start(bf16[8,256,128]{2,1,0:T(8,128)(2,1)} %bitcast.16.after_ref), calls=%async_computation.2 | async-start | bytes 1048576 | tf_op jit(solution)/shard_map/all_to_all | solution.py:346
  74.0 18.1 %copy-start.10 = (bf16[8,48,512]{2,1,0:T(8,128)(2,1)S(1)}, bf16[8,48,512]{2,1,0:T(8,128)(2,1)}, u32[]{:S(2)}) copy-start(bf16[8,48,512]{2,1,0:T(8,128)(2,1)} %get-tuple-element.59) | copy-start | bytes 1179652
  74.0 14.8 %collective-permute-start.16 = (bf16[4,48,512]{2,1,0:T(8,128)(2,1)S(1)}, bf16[4,48,512]{2,1,0:T(8,128)(2,1)S(1)}, u32[]{:S(2)}, u32[]{:S(2)}) collective-permute-start(bf16[4,48,512]{2,1,0:T(8,128)(2,1)S(1)} %copy-done.26), channel_id=1, source_target_pairs={{0,6},{1,7},{2,0},{3,1},{4,2},{5,3},{6,4},{7,5},{8,14},{9,15},{10,... | collective-permute-start | bytes 589832 | tf_op jit(solution)/shard_map/ppermute | solution.py:39
  76.8 26.4 %collective-permute-start.14 = (bf16[8,48,512]{2,1,0:T(8,128)(2,1)}, bf16[8,48,512]{2,1,0:T(8,128)(2,1)S(1)}, u32[]{:S(2)}, u32[]{:S(2)}) collective-permute-start(bf16[8,48,512]{2,1,0:T(8,128)(2,1)} %get-tuple-element.61), channel_id=1, source_target_pairs={{0,2},{1,3},{2,4},{3,5},{4,6},{5,7},{6,0},{7,1},{8,10},{9,11},{10,... | collective-permute-start | bytes 1179656 | tf_op jit(solution)/shard_map/ppermute | solution.py:36
  76.8 15.3 %collective-permute-start.12 = (bf16[4,48,512]{2,1,0:T(8,128)(2,1)S(1)}, bf16[4,48,512]{2,1,0:T(8,128)(2,1)S(1)}, u32[]{:S(2)}, u32[]{:S(2)}) collective-permute-start(bf16[4,48,512]{2,1,0:T(8,128)(2,1)S(1)} %copy-done.24), channel_id=1, source_target_pairs={{0,2},{1,3},{2,4},{3,5},{4,6},{5,7},{6,0},{7,1},{8,10},{9,11},{10,... | collective-permute-start | bytes 589832 | tf_op jit(solution)/shard_map/ppermute | solution.py:36
  76.8 45.9 %collective-permute-start.11 = (bf16[8,48,512]{2,1,0:T(8,128)(2,1)}, bf16[8,48,512]{2,1,0:T(8,128)(2,1)}, u32[]{:S(2)}, u32[]{:S(2)}) collective-permute-start(bf16[8,48,512]{2,1,0:T(8,128)(2,1)} %get-tuple-element.57), channel_id=1, source_target_pairs={{0,6},{1,7},{2,0},{3,1},{4,2},{5,3},{6,4},{7,5},{8,14},{9,15},{10,... | collective-permute-start | bytes 1179656 | tf_op jit(solution)/shard_map/ppermute | solution.py:39
  89.6 11.3 %collective-permute-start.17 = (bf16[8,48,512]{2,1,0:T(8,128)(2,1)}, bf16[8,48,512]{2,1,0:T(8,128)(2,1)}, u32[]{:S(2)}, u32[]{:S(2)}) collective-permute-start(bf16[8,48,512]{2,1,0:T(8,128)(2,1)} %add_convert_fusion.2), channel_id=1, source_target_pairs={{0,6},{1,7},{2,0},{3,1},{4,2},{5,3},{6,4},{7,5},{8,14},{9,15},{10,... | collective-permute-start | bytes 1179656 | tf_op jit(solution)/shard_map/ppermute | solution.py:39
  92.9 10.3 %collective-permute-start.13 = (bf16[8,48,512]{2,1,0:T(8,128)(2,1)}, bf16[8,48,512]{2,1,0:T(8,128)(2,1)S(1)}, u32[]{:S(2)}, u32[]{:S(2)}) collective-permute-start(bf16[8,48,512]{2,1,0:T(8,128)(2,1)} %add_convert_fusion.4), channel_id=1, source_target_pairs={{0,1},{1,0},{2,3},{3,2},{4,5},{5,4},{6,7},{7,6},{8,9},{9,8},{10,11... | collective-permute-start | bytes 1179656 | tf_op jit(solution)/shard_map/ppermute | solution.py:42
  94.0 19.6 %all-to-all-start.3 = ((bf16[8,352,128]{2,1,0:T(8,128)(2,1)}), bf16[8,352,128]{2,1,0:T(8,128)(2,1)S(1)}, u32[]{:S(2)}, u32[]{:S(2)}) async-start(bf16[8,352,128]{2,1,0:T(8,128)(2,1)} %pad_maximum_fusion.1), calls=%async_computation.3 | async-start | bytes 1441792 | tf_op jit(solution)/shard_map/all_to_all | solution.py:346
  102.7 19.9 %collective-permute-start.18 = (bf16[8,48,512]{2,1,0:T(8,128)(2,1)}, bf16[8,48,512]{2,1,0:T(8,128)(2,1)}, u32[]{:S(2)}, u32[]{:S(2)}) collective-permute-start(bf16[8,48,512]{2,1,0:T(8,128)(2,1)} %add_convert_fusion.1), channel_id=1, source_target_pairs={{0,1},{1,0},{2,3},{3,2},{4,5},{5,4},{6,7},{7,6},{8,9},{9,8},{10,11... | collective-permute-start | bytes 1179656 | tf_op jit(solution)/shard_map/ppermute | solution.py:42
  104.1 18.5 %collective-permute-start.15 = (bf16[8,48,512]{2,1,0:T(8,128)(2,1)}, bf16[8,48,512]{2,1,0:T(8,128)(2,1)}, u32[]{:S(2)}, u32[]{:S(2)}) collective-permute-start(bf16[8,48,512]{2,1,0:T(8,128)(2,1)} %add_convert_fusion.3), channel_id=1, source_target_pairs={{0,2},{1,3},{2,4},{3,5},{4,6},{5,7},{6,0},{7,1},{8,10},{9,11},{10,... | collective-permute-start | bytes 1179656 | tf_op jit(solution)/shard_map/ppermute | solution.py:36
  104.4 18.3 %copy-start.5 = (bf16[8,48,512]{2,1,0:T(8,128)(2,1)S(1)}, bf16[8,48,512]{2,1,0:T(8,128)(2,1)}, u32[]{:S(2)}) copy-start(bf16[8,48,512]{2,1,0:T(8,128)(2,1)} %get-tuple-element.56.after_ref) | copy-start | bytes 1179652
  113.6 3.2 %collective-permute-start.10 = (bf16[8,96,128]{2,1,0:T(8,128)(2,1)S(1)}, bf16[8,96,128]{2,1,0:T(8,128)(2,1)S(1)}, u32[]{:S(2)}, u32[]{:S(2)}) collective-permute-start(bf16[8,96,128]{2,1,0:T(8,128)(2,1)S(1)} %slice.21.own_ref), channel_id=1, source_target_pairs={{0,64},{64,0},{1,65},{65,1},{2,66},{66,2},{3,67},{67,3},{4,68},{68... | collective-permute-start | bytes 589832 | tf_op jit(solution)/shard_map/ppermute | solution.py:342
  116.4 14.7 %collective-permute-start.19 = (bf16[2048,128]{1,0:T(8,128)(2,1)S(1)}, bf16[2048,128]{1,0:T(8,128)(2,1)}, u32[]{:S(2)}, u32[]{:S(2)}) collective-permute-start(bf16[2048,128]{1,0:T(8,128)(2,1)S(1)} %bitcast.39), channel_id=1, source_target_pairs={{0,64},{64,0},{1,65},{65,1},{2,66},{66,2},{3,67},{67,3},{4,68},{68... | collective-permute-start | bytes 1572872 | tf_op jit(solution)/shard_map/ppermute | solution.py:342
  119.3 10.9 %all-to-all-start.4 = ((bf16[8,96,128]{2,1,0:T(8,128)(2,1)}), bf16[8,96,128]{2,1,0:T(8,128)(2,1)S(1)}, u32[]{:S(2)}, u32[]{:S(2)}) async-start(bf16[8,96,128]{2,1,0:T(8,128)(2,1)} %pick.3), calls=%async_computation.4 | async-start | bytes 393216 | tf_op jit(solution)/shard_map/all_to_all | solution.py:346
  (20 other events, 136.0 us)
